TPU v7x, 512 devices: a whole 4x8x8 slice. The times are simulated.
512 devices in a mesh: row: 64 (over z_hi, y, core), col: 8 (over z_lo, x).
Axes of the slice: x: 4, y: 8, z: 8 (z_hi: 4, z_lo: 2; z = z_hi * 2 + z_lo), core: 2. Of those that a mesh axis runs over, the one named last changes fastest.
Arguments:
- left: bfloat16 [1024, 49152], P('col', 'row'), may hold values from -0.02734375 to 0.02734375
- right: bfloat16 [49152, 4096], P('row', 'col'), may hold values from -6 to 6
- occupancy: int32 [16, 768], P('col', 'row'), may hold values from 0 to 1
- owners: int32 [8], replicated, may hold values from 0 to 7
- slab: bfloat16 [8, 128, 4096], P(None, 'row', 'col'), may hold values from -6 to 6
Outputs:
- updated: float32 [8, 128, 4096], P(None, 'row', 'col')
All inputs are finite; a program needn't handle non-finite values.
Results may differ from a plain program's by a relative error of at most 0.0005.
Values may be sent and summed in bfloat16 or wider, within the bound.
No kernel may reach another device: no remote copies, remote signals or barrier semaphores. Data moves between devices by JAX's collectives and lax.ppermute only.
A program may use at most 64 MiB of HBM per device.

v0:
```python
import functools

import jax
import jax.numpy as jnp
from jax import lax
from jax.experimental import pallas as pl
from jax.experimental.pallas import tpu as pltpu
from jax.sharding import Mesh, PartitionSpec as P

ATOM_BLOCK = 64
PANEL_ROWS = 128
HALF = 64
SLOTS = 8
LANES = 128
TILE = 8
DISTINCT = (4, 5, 6, 8)
LAST = 4
MEMBERS = [(member - LAST) % 32 for member in range(32)]
COLUMNS = [6, 7, 0, 1, 2, 3, 4, 5]
SHARERS = [core * 8 + column for core in range(2) for column in COLUMNS]
PACKED_ROWS = SLOTS // 2 * 32
LIST_ROWS = 16
WIRE = jnp.float16
WIRE_SCALE = 128.0


def row_order():
    place = lax.broadcasted_iota(jnp.int32, (PANEL_ROWS, PANEL_ROWS), 0)
    row = lax.broadcasted_iota(jnp.int32, (PANEL_ROWS, PANEL_ROWS), 1)
    core, at, b = place // HALF, (place % HALF) // 2, place % 2
    return (row == at * 4 + core * 2 + b).astype(jnp.bfloat16)


def pack_kernel(marks_ref, left_ref, out_ref, rows, tiles):
    rows[...] = jnp.dot(row_order(), left_ref[...], preferred_element_type=jnp.float32).astype(jnp.bfloat16)
    tiles[...] = jnp.zeros_like(tiles)
    lane = lax.broadcasted_iota(jnp.int32, (32, LANES), 1)
    list_lane = lax.broadcasted_iota(jnp.int32, (LIST_ROWS, LANES), 1)
    block_rows, block_cols = marks_ref.shape
    count = jnp.int32(0)
    listed = jnp.zeros((LIST_ROWS, LANES), jnp.float32)
    for i in range(block_rows):
        for j in range(block_cols):
            kept = marks_ref[i, j] != 0
            slot = jnp.minimum(count, SLOTS - 1)
            fits = jnp.logical_and(kept, count < SLOTS)

            @pl.when(fits)
            def _(i=i, j=j, slot=slot):
                side = lax.rem(slot, 2)
                here = lane // ATOM_BLOCK == side
                at = pl.ds(pl.multiple_of(lax.div(slot, 2) * 32, 32), 32)
                for half in range(2):
                    block = rows[half * HALF + i * 32 : half * HALF + i * 32 + 32, j // 2 * LANES : (j // 2 + 1) * LANES]
                    turned = pltpu.roll(block, ATOM_BLOCK, 1)
                    placed = jnp.where(side == j % 2, block, turned)
                    tiles[half, at, :] = jnp.where(here, placed, tiles[half, at, :])

            mark = jnp.where(fits, 1.0, 0.0)
            listed = listed + jnp.where(list_lane == slot, mark * i, 0.0)
            listed = listed + jnp.where(list_lane == slot + 16, mark * j, 0.0)
            count = count + kept.astype(jnp.int32)
    listed = listed + jnp.where(list_lane == 32, count.astype(jnp.float32), 0.0)
    for to in range(out_ref.shape[0]):
        out_ref[to, :PACKED_ROWS, :] = tiles[to // 8]
        out_ref[to, PACKED_ROWS:, :] = listed.astype(jnp.bfloat16)


def destination_order(places, row_of_owners, slots):
    place = lax.broadcasted_iota(jnp.int32, (32 * slots, 1), 0)
    at = sum((place >= k * 2 * slots).astype(jnp.int32) for k in range(1, 16))
    slot, b = (place - at * (2 * slots)) // 2, place % 2
    wanted = at * 2 + b
    filled = jnp.int32(0)
    owners = [places[row_of_owners, t] for t in range(8)]
    for panel in range(8):
        owned = functools.reduce(jnp.logical_or, [owner == panel for owner in owners])
        wanted = wanted + jnp.where(slot == jnp.where(owned, filled, slots), panel * 32, 0)
        filled = filled + owned.astype(jnp.int32)
    row = lax.broadcasted_iota(jnp.int32, (32 * slots, 256), 1)
    return (row == wanted).astype(jnp.bfloat16)


def product_kernel(slots, facts_ref, got_ref, right_ref, right2_ref, out_ref, flag_ref, dense, ordered, lists, places, sem):
    sources = got_ref.shape[0]
    depth = right_ref.shape[0]
    lists[sources : sources + 1, :] = facts_ref[...]
    for source in range(sources):
        lists[source : source + 1, :] = got_ref[source, PACKED_ROWS : PACKED_ROWS + 1, :].astype(jnp.int32)
    copy = pltpu.make_async_copy(lists, places, sem)
    copy.start()
    dense[...] = jnp.zeros_like(dense)
    copy.wait()
    core = places[sources, 8]
    order = destination_order(places, sources, slots)
    side_of_lane = lax.broadcasted_iota(jnp.int32, (32, LANES), 1) // ATOM_BLOCK

    def put(source, first, slots_here):
        for slot in slots_here:
            i = places[source, slot]
            j = places[source, slot + 16]
            block = got_ref[source, slot // 2 * 32 : slot // 2 * 32 + 32, :]
            turned = pltpu.roll(block, ATOM_BLOCK, 1)
            side = lax.rem(j, 2)
            placed = jnp.where(side == slot % 2, block, turned)
            to_rows = pl.ds(pl.multiple_of(i * 256 + COLUMNS[source % 8] * 32, 32), 32)
            to_lanes = pl.ds(pl.multiple_of(first + lax.div(j, 2) * LANES, LANES), LANES)
            here = side_of_lane == jnp.where(slot < places[source, 32], side, 2)
            dense[to_rows, to_lanes] = jnp.where(here, placed, dense[to_rows, to_lanes])

    firsts = [jnp.where(core == source // 8, 0, depth) for source in range(sources)]
    for source in range(sources):
        put(source, firsts[source], range(SLOTS // 2))
    most = jnp.int32(0)
    for source in range(sources):
        most = jnp.maximum(most, places[source, 32])

        @pl.when(places[source, 32] > SLOTS // 2)
        def _(source=source):
            put(source, firsts[source], range(SLOTS // 2, SLOTS))

    flag_ref[0] = (most > SLOTS).astype(jnp.int32)

    size = 32 * slots
    for i in range(2):
        ordered[i * size : i * size + size, :] = jnp.dot(
            order, dense[i * 256 : i * 256 + 256, :], preferred_element_type=jnp.float32
        ).astype(jnp.bfloat16)
    sums = jnp.dot(ordered[:, :depth], right_ref[...], preferred_element_type=jnp.float32) + jnp.dot(
        ordered[:, depth:], right2_ref[...], preferred_element_type=jnp.float32
    )
    parts = sums.shape[1] // LANES
    first = LAST * 2 * slots
    for q in range(parts):
        columns = sums[:, q * LANES : (q + 1) * LANES]
        out_ref[pl.ds(q, first, stride=parts), :] = columns[2 * size - first :]
        out_ref[pl.ds(first * parts + q, 2 * size - first, stride=parts), :] = columns[: 2 * size - first]


def pack(marks, left):
    return pl.pallas_call(
        pack_kernel,
        out_shape=jax.ShapeDtypeStruct((16, PACKED_ROWS + LIST_ROWS, LANES), jnp.bfloat16),
        in_specs=[pl.BlockSpec(memory_space=pltpu.SMEM), pl.BlockSpec(memory_space=pltpu.VMEM)],
        out_specs=pl.BlockSpec(memory_space=pltpu.VMEM),
        scratch_shapes=[
            pltpu.VMEM(left.shape, jnp.bfloat16),
            pltpu.VMEM((2, PACKED_ROWS, LANES), jnp.bfloat16),
        ],
    )(marks, left)


def unpack_product(slots, facts, got, right, right2):
    depth, width = right.shape
    return pl.pallas_call(
        functools.partial(product_kernel, slots),
        out_shape=[
            jax.ShapeDtypeStruct((32 * slots * 2 * (width // LANES), LANES), jnp.float32),
            jax.ShapeDtypeStruct((1,), jnp.int32),
        ],
        in_specs=[pl.BlockSpec(memory_space=pltpu.VMEM)] * 4,
        out_specs=[pl.BlockSpec(memory_space=pltpu.VMEM), pl.BlockSpec(memory_space=pltpu.SMEM)],
        scratch_shapes=[
            pltpu.VMEM((512, 2 * depth), jnp.bfloat16),
            pltpu.VMEM((64 * slots, 2 * depth), jnp.bfloat16),
            pltpu.VMEM((24, LANES), jnp.int32),
            pltpu.SMEM((24, LANES), jnp.int32),
            pltpu.SemaphoreType.DMA,
        ],
        compiler_params=pltpu.CompilerParams(vmem_limit_bytes=24 * 2**20),
        cost_estimate=pl.CostEstimate(flops=2 * 512 * 2 * depth * width, bytes_accessed=4 * 2**20, transcendentals=0),
    )(facts, got, right, right2)


def spread_marks(marks):
    values = marks.astype(jnp.bfloat16)
    count_r, count_c = values.shape
    return jnp.broadcast_to(
        values[:, None, :, None], (count_r, ATOM_BLOCK, count_c, ATOM_BLOCK)
    ).reshape(count_r * ATOM_BLOCK, count_c * ATOM_BLOCK)


def dense_product(slots, core, owners, left, right, right2, occupancy):
    depth, width = right.shape
    kept = left * spread_marks(occupancy)
    halves = jnp.dot(row_order(), kept, preferred_element_type=jnp.float32).astype(jnp.bfloat16)
    sent = jnp.broadcast_to(halves.reshape(2, 1, HALF, depth), (2, 8, HALF, depth)).reshape(16, HALF, depth)
    panels = lax.all_to_all(sent, ("core", "zlo", "x"), 0, 0, tiled=True).reshape(2, 8 * HALF, depth)
    own = lax.dynamic_index_in_dim(panels, core, 0, keepdims=False)
    other = lax.dynamic_index_in_dim(panels, 1 - core, 0, keepdims=False)
    product = jnp.dot(own, right, preferred_element_type=jnp.float32) + jnp.dot(
        other, right2, preferred_element_type=jnp.float32
    )
    number = jnp.arange(8)
    owned = jnp.any(owners[:, None] == number[None, :], axis=0)
    before = jnp.sum(owned[:, None] & (number[:, None] < number[None, :]), axis=0)
    panel_of_slot = jnp.sum(jnp.where(owned[None, :] & (before[None, :] == number[:slots, None]), number[None, :], 0), axis=1)
    chosen = jnp.take(product.reshape(8, 32, 2 * width // LANES, LANES), panel_of_slot, axis=0)
    return lax.optimization_barrier(jnp.roll(chosen.transpose(1, 0, 2, 3), LAST, axis=0).reshape(-1, LANES))


def update(slab, chosen, sums):
    picked = jnp.sum(jnp.where(chosen.reshape(chosen.shape + (1,) * (sums.ndim - 1)), sums[None], 0.0), axis=1)
    return 1.5 * slab.astype(jnp.float32) - 0.5 * picked.reshape(slab.shape)


def body(left, right, occupancy, owners, slab):
    core = lax.axis_index("core")
    panels = jnp.arange(8)

    right2 = lax.ppermute(right, "core", [(0, 1), (1, 0)])
    packed, owners = lax.optimization_barrier((pack(occupancy, left), owners))
    got = lax.all_to_all(packed, ("core", "zlo", "x"), 0, 0, axis_index_groups=[SHARERS], tiled=True)

    owned = jnp.any(owners[:, None] == panels[None, :], axis=0)
    number = jnp.sum(owned)
    slot_of_step = jnp.sum(owned[None, :] & (panels[None, :] < owners[:, None]), axis=1)

    facts = jnp.pad(jnp.concatenate([owners, core.reshape(1)]), (0, LANES - 9)).reshape(1, LANES)

    def reduced(slots):
        def branch():
            def to_wire(product):
                return (product * WIRE_SCALE).astype(WIRE).reshape(32, slots, TILE, LANES)

            product, flag = unpack_product(slots, facts, got, right, right2)
            parts = to_wire(product)
            parts = lax.switch(
                flag[0],
                [lambda: parts, lambda: to_wire(dense_product(slots, core, owners, left, right, right2, occupancy))],
            )
            came = lax.all_to_all(parts, ("zhi", "y"), 0, 0, axis_index_groups=[MEMBERS], tiled=True)
            sums = jnp.sum(came.astype(jnp.float32), axis=0) * (1.0 / WIRE_SCALE)
            return update(slab, slot_of_step[:, None] == jnp.arange(slots)[None, :], sums)

        return branch

    which = sum((number > slots).astype(jnp.int32) for slots in DISTINCT[:-1])
    return lax.switch(which, [reduced(slots) for slots in DISTINCT])


def solution(mesh):
    fine = Mesh(mesh.devices.reshape(4, 8, 2, 2, 4), ("zhi", "y", "core", "zlo", "x"))
    row, col = ("zhi", "y", "core"), ("zlo", "x")
    in_specs = (P(col, row), P(row, col), P(col, row), P(), P(None, row, col))
    out_specs = P(None, row, col)
    return jax.shard_map(body, mesh=fine, in_specs=in_specs, out_specs=out_specs, check_vma=False)
```

profile of v0, /device:TPU:1, one launch (start us, length us, event | category | flops | bytes accessed | tf_op | source)
XLA Modules:
  0.0 53.7 jit_solution(8822318863090856609)
XLA Ops:
  0.0 0.0 copy-start.4
  0.0 0.0 copy-start.1
  0.0 0.0 copy-start.5
  0.0 0.0 copy-start
  0.0 0.0 copy-start.2
  0.0 2.3 %shard_map.63 = bf16[16,144,128]{2,1,0:T(8,128)(2,1)} custom-call(s32[2,12]{1,0:T(2,128)} %marks_ref.1, bf16[128,768]{1,0:T(8,128)(2,1)} %left_ref.1), custom_call_target="tpu_custom_call" | custom-call | tf_op jit(solution)/shard_map/pallas_call | solution.py:141
  2.3 12.3 %all-to-all-start.8 = ((bf16[16,144,128]{2,1,0:T(8,128)(2,1)}), bf16[16,144,128]{2,1,0:T(8,128)(2,1)S(1)}, u32[]{:S(2)}, u32[]{:S(2)}) async-start(bf16[16,144,128]{2,1,0:T(8,128)(2,1)} %shard_map.63), calls=%async_computation.8 | async-start | bytes 1179648 | tf_op jit(solution)/shard_map/all_to_all | solution.py:213
  14.6 0.0 copy-done
  14.6 2.3 %collective-permute-start = (bf16[768,512]{1,0:T(8,128)(2,1)S(1)}, bf16[768,512]{1,0:T(8,128)(2,1)S(1)}, u32[]{:S(2)}, u32[]{:S(2)}) collective-permute-start(bf16[768,512]{1,0:T(8,128)(2,1)S(1)} %copy-done), channel_id=1, source_target_pairs={{0,8},{8,0},{1,9},{9,1},{2,10},{10,2},{3,11},{11,3},{4,12},{12,4},... | collective-permute-start | bytes 2359304 | tf_op jit(solution)/shard_map/ppermute | solution.py:211
  16.9 0.0 copy-done.5
  16.9 0.1 fusion.169
  17.0 0.6 %convert_reduce_fusion.8 = s32[]{:T(128)} fusion(pred[8]{0:T(512)(128)(4,1)S(1)} %fusion.169), kind=kLoop, calls=%fused_computation.320 | loop fusion | flops 15 | bytes 12 | tf_op jit(solution)/shard_map/reduce_sum | solution.py:216
  19.6 0.1 pad_add_fusion
  19.7 0.1 fusion.171
  19.8 0.0 collective-permute-done
  19.8 2.9 %all-to-all-done.8 = bf16[16,144,128]{2,1,0:T(8,128)(2,1)S(1)} async-done(((bf16[16,144,128]{2,1,0:T(8,128)(2,1)}), bf16[16,144,128]{2,1,0:T(8,128)(2,1)S(1)}, u32[]{:S(2)}, u32[]{:S(2)}) %all-to-all-start.8) | async-done | bytes 589856 | tf_op jit(solution)/shard_map/all_to_all | solution.py:213
  22.6 0.0 copy-done.4
  22.6 0.0 copy-done.1
  22.6 0.0 copy-done.2
  22.6 30.5 %conditional.5 = (f32[8,2,512]{2,1,0:T(2,128)S(1)}) conditional(s32[]{:T(128)} %clamp.27, (bf16[8,2,512]{2,1,0:T(2,128)(2,1)S(1)}, s32[8,8]{1,0:T(8,128)S(1)}, s32[9]{0:T(128)S(1)}, bf16[16,144,128]{2,1,0:T(8,128)(2,1)S(1)}, bf16[768,512]{1,0:T(8,128)(2,1)S(1)}, /*index=5*/bf16[768,512]{1,0:T(8,128)(2,1)S(1)}, ...), branch_computations={%region_3.11_spmd, %region_11.19_spmd, %region_19.27_spmd, %region... | conditional | flops 1638871552 | bytes 36762268 | solution.py:239
  22.9 2.9 %branch_2_fun.1 = (f32[1536,128]{1,0:T(8,128)S(1)}, s32[1]{0:T(128)}) custom-call(s32[1,128]{1,0:T(1,128)S(1)} %pad_bitcast_fusion.2.facts_ref, bf16[16,144,128]{2,1,0:T(8,128)(2,1)S(1)} %get-tuple-element.211.got_ref, bf16[768,512]{1,0:T(8,128)(2,1)S(1)} %get-tuple-element.212.right_ref, bf16[768,512]{1,0:T(8,128)(2,1)S(1)} %get-tuple-element.213.right2_ref), custom_call_target="tpu_custom_call" | custom-call | flops 805306368 | bytes 4194304 | tf_op jit(solution)/shard_map/cond/branch_2_fun/pallas_call | solution.py:155
  25.8 0.8 %multiply_convert_fusion.5 = f16[1536,128]{1,0:T(8,128)(2,1)} fusion(f32[1536,128]{1,0:T(8,128)S(1)} %get-tuple-element.215), kind=kLoop, calls=%fused_computation.228 | loop fusion | flops 393216 | bytes 1179648 | tf_op jit(solution)/shard_map/cond/branch_2_fun/convert_element_type | solution.py:224
  27.3 13.9 %all-to-all-start.5 = ((f16[32,6,8,128]{3,2,1,0:T(8,128)(2,1)}), f16[32,6,8,128]{3,2,1,0:T(8,128)(2,1)S(1)}, u32[]{:S(2)}, u32[]{:S(2)}) async-start(f16[32,6,8,128]{3,2,1,0:T(8,128)(2,1)} %bitcast.35), calls=%async_computation.5 | async-start | bytes 786432 | tf_op jit(solution)/shard_map/cond/branch_2_fun/all_to_all | solution.py:232
  41.1 0.1 reduce_sum.174
  41.3 0.1 iota_compare_fusion.8
  41.3 11.0 %all-to-all-done.5 = f16[32,6,8,128]{3,2,1,0:T(8,128)(2,1)S(1)} async-done(((f16[32,6,8,128]{3,2,1,0:T(8,128)(2,1)}), f16[32,6,8,128]{3,2,1,0:T(8,128)(2,1)S(1)}, u32[]{:S(2)}, u32[]{:S(2)}) %all-to-all-start.5) | async-done | bytes 393248 | tf_op jit(solution)/shard_map/cond/branch_2_fun/all_to_all | solution.py:232
  52.4 0.1 convert_reduce_fusion.5
  52.4 0.1 select_reduce_fusion.5
  53.1 0.0 copy-start.3
  53.1 0.6 %copy-done.3 = f32[8,2,512]{2,1,0:T(2,128)} copy-done((f32[8,2,512]{2,1,0:T(2,128)}, f32[8,2,512]{2,1,0:T(2,128)S(1)}, u32[]{:S(2)}) %copy-start.3) | copy-done | bytes 32792
  (6 shorter events, 0.1 us)
Async XLA Ops:
  0.0 22.6 %copy-start.4 = (s32[2,12]{1,0:T(2,128)S(1)}, s32[2,12]{1,0:T(2,128)}, u32[]{:S(2)}) copy-start(s32[2,12]{1,0:T(2,128)} %marks_ref.1) | copy-start | bytes 292
  0.0 22.6 %copy-start.1 = (bf16[128,768]{1,0:T(8,128)(2,1)S(1)}, bf16[128,768]{1,0:T(8,128)(2,1)}, u32[]{:S(2)}) copy-start(bf16[128,768]{1,0:T(8,128)(2,1)} %left_ref.1) | copy-start | bytes 589828
  0.0 16.9 %copy-start.5 = (s32[8]{0:T(128)S(1)}, s32[8]{0:T(128)}, u32[]{:S(2)}) copy-start(s32[8]{0:T(128)} %param.20) | copy-start | bytes 100
  0.0 14.6 %copy-start = (bf16[768,512]{1,0:T(8,128)(2,1)S(1)}, bf16[768,512]{1,0:T(8,128)(2,1)}, u32[]{:S(2)}) copy-start(bf16[768,512]{1,0:T(8,128)(2,1)} %param.18) | copy-start | bytes 2359300
  0.0 22.6 %copy-start.2 = (bf16[8,2,512]{2,1,0:T(2,128)(2,1)S(1)}, bf16[8,2,512]{2,1,0:T(2,128)(2,1)}, u32[]{:S(2)}) copy-start(bf16[8,2,512]{2,1,0:T(2,128)(2,1)} %param.21) | copy-start | bytes 49156
  2.3 20.3 %all-to-all-start.8 = ((bf16[16,144,128]{2,1,0:T(8,128)(2,1)}), bf16[16,144,128]{2,1,0:T(8,128)(2,1)S(1)}, u32[]{:S(2)}, u32[]{:S(2)}) async-start(bf16[16,144,128]{2,1,0:T(8,128)(2,1)} %shard_map.63), calls=%async_computation.8 | async-start | bytes 1179648 | tf_op jit(solution)/shard_map/all_to_all | solution.py:213
  14.6 5.1 %collective-permute-start = (bf16[768,512]{1,0:T(8,128)(2,1)S(1)}, bf16[768,512]{1,0:T(8,128)(2,1)S(1)}, u32[]{:S(2)}, u32[]{:S(2)}) collective-permute-start(bf16[768,512]{1,0:T(8,128)(2,1)S(1)} %copy-done), channel_id=1, source_target_pairs={{0,8},{8,0},{1,9},{9,1},{2,10},{10,2},{3,11},{11,3},{4,12},{12,4},... | collective-permute-start | bytes 2359304 | tf_op jit(solution)/shard_map/ppermute | solution.py:211
  27.3 25.1 %all-to-all-start.5 = ((f16[32,6,8,128]{3,2,1,0:T(8,128)(2,1)}), f16[32,6,8,128]{3,2,1,0:T(8,128)(2,1)S(1)}, u32[]{:S(2)}, u32[]{:S(2)}) async-start(f16[32,6,8,128]{3,2,1,0:T(8,128)(2,1)} %bitcast.35), calls=%async_computation.5 | async-start | bytes 786432 | tf_op jit(solution)/shard_map/cond/branch_2_fun/all_to_all | solution.py:232
  53.1 0.6 %copy-start.3 = (f32[8,2,512]{2,1,0:T(2,128)}, f32[8,2,512]{2,1,0:T(2,128)S(1)}, u32[]{:S(2)}) copy-start(f32[8,2,512]{2,1,0:T(2,128)S(1)} %get-tuple-element.428) | copy-start | bytes 98308
where the time goes:
time: 54.1 us; the launch traced here: 53.7 us
  starting transfers between devices  28.4 us (52%)
  waiting for transfers between devices  13.9 us (26%)
  Pallas kernels  5.17 us (10%)
  other arithmetic  2.11 us (4%)
  between operations  2.02 us (4%)
  loops' own time  1.45 us (3%)
  local copies, waits for them, and re-layouts  0.65 us (1%)
    all_to_all x1, starting transfers between devices, branch(): lax.all_to_all(parts, ('zhi', 'y'), 0, 0, axis_index_groups=[MEMBERS], ti...  13.9 us
    all_to_all x1, starting transfers between devices, body(): lax.all_to_all(packed, ('core', 'zlo', 'x'), 0, 0, axis_index_groups=[SHA...  12.3 us
    all_to_all x1, waiting for transfers between devices, branch(): lax.all_to_all(parts, ('zhi', 'y'), 0, 0, axis_index_groups=[MEMBERS], ti...  11 us
    all_to_all x1, waiting for transfers between devices, body(): lax.all_to_all(packed, ('core', 'zlo', 'x'), 0, 0, axis_index_groups=[SHA...  2.88 us
    pallas_call x1, Pallas kernels, unpack_product(): pl.pallas_call(functools.partial(product_kernel, slots), out_shape=[jax.S...  2.85 us
    pallas_call x1, Pallas kernels, pack(): pl.pallas_call(pack_kernel, out_shape=jax.ShapeDtypeStruct((16, PACKED_RO...  2.31 us
    ppermute x1, starting transfers between devices, body(): right2 = lax.ppermute(right, 'core', [(0, 1), (1, 0)])  2.27 us
    another operation x1, loops' own time, body(): return lax.switch(which, [reduced(slots) for slots in DISTINCT])  1.44 us
  transfers between devices with their start and end apart: 3, of which 2 were waited for; matrix products, arithmetic and copies ran while one was open for 2% of the time, Pallas kernels for 0%

commit v1 on v0

--- a/solution.py
+++ b/solution.py
@@ -13,7 +13,7 @@
 SLOTS = 8
 LANES = 128
 TILE = 8
-DISTINCT = (4, 5, 6, 8)
+DISTINCT = (5, 6, 8)
 LAST = 4
 MEMBERS = [(member - LAST) % 32 for member in range(32)]
 COLUMNS = [6, 7, 0, 1, 2, 3, 4, 5]
@@ -86,7 +86,7 @@
     depth = right_ref.shape[0]
     lists[sources : sources + 1, :] = facts_ref[...]
     for source in range(sources):
-        lists[source : source + 1, :] = got_ref[source, PACKED_ROWS : PACKED_ROWS + 1, :].astype(jnp.int32)
+        lists[source : source + 1, :] = got_ref[source, PACKED_ROWS:, :].astype(jnp.int32)[:1]
     copy = pltpu.make_async_copy(lists, places, sem)
     copy.start()
     dense[...] = jnp.zeros_like(dense)

time: 54.1 us -> 53.4 us (0.987)
  waiting for transfers between devices: 13.9 us -> 14.6 us
  between operations: 2.02 us -> 1.38 us
    all_to_all x1, waiting for transfers between devices: 2.88 us -> 3.52 us  [body(): lax.all_to_all(packed, ('core', 'zlo', 'x'), 0, 0, axis_index_groups=[SHA...]
where the time goes in v1:
time: 53.4 us; the launch traced here: 53 us
  starting transfers between devices  28.3 us (53%)
  waiting for transfers between devices  14.6 us (27%)
  Pallas kernels  5.07 us (9%)
  other arithmetic  2.11 us (4%)
  between operations  1.38 us (3%)
  loops' own time  0.95 us (2%)
  local copies, waits for them, and re-layouts  0.65 us (1%)
    all_to_all x1, starting transfers between devices, branch(): lax.all_to_all(parts, ('zhi', 'y'), 0, 0, axis_index_groups=[MEMBERS], ti...  13.9 us
    all_to_all x1, starting transfers between devices, body(): lax.all_to_all(packed, ('core', 'zlo', 'x'), 0, 0, axis_index_groups=[SHA...  12.2 us
    all_to_all x1, waiting for transfers between devices, branch(): lax.all_to_all(parts, ('zhi', 'y'), 0, 0, axis_index_groups=[MEMBERS], ti...  11 us
    all_to_all x1, waiting for transfers between devices, body(): lax.all_to_all(packed, ('core', 'zlo', 'x'), 0, 0, axis_index_groups=[SHA...  3.52 us
    pallas_call x1, Pallas kernels, unpack_product(): pl.pallas_call(functools.partial(product_kernel, slots), out_shape=[jax.S...  2.62 us
    pallas_call x1, Pallas kernels, pack(): pl.pallas_call(pack_kernel, out_shape=jax.ShapeDtypeStruct((16, PACKED_RO...  2.44 us
    ppermute x1, starting transfers between devices, body(): right2 = lax.ppermute(right, 'core', [(0, 1), (1, 0)])  2.27 us
  transfers between devices with their start and end apart: 3, of which 2 were waited for; matrix products, arithmetic and copies ran while one was open for 2% of the time, Pallas kernels for 0%

profile of v1, /device:TPU:1, one launch (start us, length us, event | category | flops | bytes accessed | tf_op | source)
XLA Modules:
  0.0 53.0 jit_solution(11782588940162794268)
XLA Ops:
  0.0 0.0 copy-start.4
  0.0 0.0 copy-start.1
  0.0 0.0 copy-start.5
  0.0 0.0 copy-start
  0.0 0.0 copy-start.2
  0.0 2.4 %shard_map.61 = bf16[16,144,128]{2,1,0:T(8,128)(2,1)} custom-call(s32[2,12]{1,0:T(2,128)} %marks_ref.1, bf16[128,768]{1,0:T(8,128)(2,1)} %left_ref.1), custom_call_target="tpu_custom_call" | custom-call | tf_op jit(solution)/shard_map/pallas_call | solution.py:141
  2.5 12.2 %all-to-all-start.6 = ((bf16[16,144,128]{2,1,0:T(8,128)(2,1)}), bf16[16,144,128]{2,1,0:T(8,128)(2,1)S(1)}, u32[]{:S(2)}, u32[]{:S(2)}) async-start(bf16[16,144,128]{2,1,0:T(8,128)(2,1)} %shard_map.61), calls=%async_computation.6 | async-start | bytes 1179648 | tf_op jit(solution)/shard_map/all_to_all | solution.py:213
  14.6 0.0 copy-done
  14.6 2.3 %collective-permute-start = (bf16[768,512]{1,0:T(8,128)(2,1)S(1)}, bf16[768,512]{1,0:T(8,128)(2,1)S(1)}, u32[]{:S(2)}, u32[]{:S(2)}) collective-permute-start(bf16[768,512]{1,0:T(8,128)(2,1)S(1)} %copy-done), channel_id=1, source_target_pairs={{0,8},{8,0},{1,9},{9,1},{2,10},{10,2},{3,11},{11,3},{4,12},{12,4},... | collective-permute-start | bytes 2359304 | tf_op jit(solution)/shard_map/ppermute | solution.py:211
  16.9 0.0 copy-done.5
  16.9 0.1 fusion.127
  17.0 0.6 %convert_reduce_fusion.6 = s32[]{:T(128)} fusion(pred[8]{0:T(512)(128)(4,1)S(1)} %fusion.127), kind=kLoop, calls=%fused_computation.242 | loop fusion | flops 15 | bytes 12 | tf_op jit(solution)/shard_map/reduce_sum | solution.py:216
  19.0 0.1 pad_add_fusion
  19.0 0.1 fusion.129
  19.1 0.0 collective-permute-done
  19.1 3.5 %all-to-all-done.6 = bf16[16,144,128]{2,1,0:T(8,128)(2,1)S(1)} async-done(((bf16[16,144,128]{2,1,0:T(8,128)(2,1)}), bf16[16,144,128]{2,1,0:T(8,128)(2,1)S(1)}, u32[]{:S(2)}, u32[]{:S(2)}) %all-to-all-start.6) | async-done | bytes 589856 | tf_op jit(solution)/shard_map/all_to_all | solution.py:213
  22.6 0.0 copy-done.4
  22.6 0.0 copy-done.1
  22.6 0.0 copy-done.2
  22.6 29.8 %conditional.4 = (f32[8,2,512]{2,1,0:T(2,128)S(1)}) conditional(s32[]{:T(128)} %clamp.21, (bf16[8,2,512]{2,1,0:T(2,128)(2,1)S(1)}, s32[8,8]{1,0:T(8,128)S(1)}, s32[9]{0:T(128)S(1)}, bf16[16,144,128]{2,1,0:T(8,128)(2,1)S(1)}, bf16[768,512]{1,0:T(8,128)(2,1)S(1)}, /*index=5*/bf16[768,512]{1,0:T(8,128)(2,1)S(1)}, s32[8]{0:T(128)S(1)}, ...), branch_computations={%region_3.11_spmd, %region_11.19_spmd, %region_19.27_spmd} | conditional | flops 1638871552 | bytes 36762268 | solution.py:239
  22.7 2.6 %branch_1_fun.1 = (f32[1536,128]{1,0:T(8,128)S(1)}, s32[1]{0:T(128)}) custom-call(s32[1,128]{1,0:T(1,128)S(1)} %pad_bitcast_fusion.1.facts_ref, bf16[16,144,128]{2,1,0:T(8,128)(2,1)S(1)} %get-tuple-element.153.got_ref, bf16[768,512]{1,0:T(8,128)(2,1)S(1)} %get-tuple-element.154.right_ref, bf16[768,512]{1,0:T(8,128)(2,1)S(1)} %get-tuple-element.155.right2_ref), custom_call_target="tpu_custom_call" | custom-call | flops 805306368 | bytes 4194304 | tf_op jit(solution)/shard_map/cond/branch_1_fun/pallas_call | solution.py:155
  25.3 0.8 %multiply_convert_fusion.3 = f16[1536,128]{1,0:T(8,128)(2,1)} fusion(f32[1536,128]{1,0:T(8,128)S(1)} %get-tuple-element.157), kind=kLoop, calls=%fused_computation.150 | loop fusion | flops 393216 | bytes 1179648 | tf_op jit(solution)/shard_map/cond/branch_1_fun/convert_element_type | solution.py:224
  26.8 13.9 %all-to-all-start.3 = ((f16[32,6,8,128]{3,2,1,0:T(8,128)(2,1)}), f16[32,6,8,128]{3,2,1,0:T(8,128)(2,1)S(1)}, u32[]{:S(2)}, u32[]{:S(2)}) async-start(f16[32,6,8,128]{3,2,1,0:T(8,128)(2,1)} %bitcast.23), calls=%async_computation.3 | async-start | bytes 786432 | tf_op jit(solution)/shard_map/cond/branch_1_fun/all_to_all | solution.py:232
  40.7 0.1 reduce_sum.135
  40.8 0.1 iota_compare_fusion.5
  40.9 11.0 %all-to-all-done.3 = f16[32,6,8,128]{3,2,1,0:T(8,128)(2,1)S(1)} async-done(((f16[32,6,8,128]{3,2,1,0:T(8,128)(2,1)}), f16[32,6,8,128]{3,2,1,0:T(8,128)(2,1)S(1)}, u32[]{:S(2)}, u32[]{:S(2)}) %all-to-all-start.3) | async-done | bytes 393248 | tf_op jit(solution)/shard_map/cond/branch_1_fun/all_to_all | solution.py:232
  51.9 0.1 convert_reduce_fusion.3
  52.0 0.1 select_reduce_fusion.3
  52.4 0.0 copy-start.3
  52.4 0.6 %copy-done.3 = f32[8,2,512]{2,1,0:T(2,128)} copy-done((f32[8,2,512]{2,1,0:T(2,128)}, f32[8,2,512]{2,1,0:T(2,128)S(1)}, u32[]{:S(2)}) %copy-start.3) | copy-done | bytes 32792
  (6 shorter events, 0.1 us)
Async XLA Ops:
  0.0 22.6 %copy-start.4 = (s32[2,12]{1,0:T(2,128)S(1)}, s32[2,12]{1,0:T(2,128)}, u32[]{:S(2)}) copy-start(s32[2,12]{1,0:T(2,128)} %marks_ref.1) | copy-start | bytes 292
  0.0 22.6 %copy-start.1 = (bf16[128,768]{1,0:T(8,128)(2,1)S(1)}, bf16[128,768]{1,0:T(8,128)(2,1)}, u32[]{:S(2)}) copy-start(bf16[128,768]{1,0:T(8,128)(2,1)} %left_ref.1) | copy-start | bytes 589828
  0.0 16.9 %copy-start.5 = (s32[8]{0:T(128)S(1)}, s32[8]{0:T(128)}, u32[]{:S(2)}) copy-start(s32[8]{0:T(128)} %param.17) | copy-start | bytes 100
  0.0 14.6 %copy-start = (bf16[768,512]{1,0:T(8,128)(2,1)S(1)}, bf16[768,512]{1,0:T(8,128)(2,1)}, u32[]{:S(2)}) copy-start(bf16[768,512]{1,0:T(8,128)(2,1)} %param.15) | copy-start | bytes 2359300
  0.0 22.6 %copy-start.2 = (bf16[8,2,512]{2,1,0:T(2,128)(2,1)S(1)}, bf16[8,2,512]{2,1,0:T(2,128)(2,1)}, u32[]{:S(2)}) copy-start(bf16[8,2,512]{2,1,0:T(2,128)(2,1)} %param.18) | copy-start | bytes 49156
  2.5 20.2 %all-to-all-start.6 = ((bf16[16,144,128]{2,1,0:T(8,128)(2,1)}), bf16[16,144,128]{2,1,0:T(8,128)(2,1)S(1)}, u32[]{:S(2)}, u32[]{:S(2)}) async-start(bf16[16,144,128]{2,1,0:T(8,128)(2,1)} %shard_map.61), calls=%async_computation.6 | async-start | bytes 1179648 | tf_op jit(solution)/shard_map/all_to_all | solution.py:213
  14.6 4.5 %collective-permute-start = (bf16[768,512]{1,0:T(8,128)(2,1)S(1)}, bf16[768,512]{1,0:T(8,128)(2,1)S(1)}, u32[]{:S(2)}, u32[]{:S(2)}) collective-permute-start(bf16[768,512]{1,0:T(8,128)(2,1)S(1)} %copy-done), channel_id=1, source_target_pairs={{0,8},{8,0},{1,9},{9,1},{2,10},{10,2},{3,11},{11,3},{4,12},{12,4},... | collective-permute-start | bytes 2359304 | tf_op jit(solution)/shard_map/ppermute | solution.py:211
  26.8 25.1 %all-to-all-start.3 = ((f16[32,6,8,128]{3,2,1,0:T(8,128)(2,1)}), f16[32,6,8,128]{3,2,1,0:T(8,128)(2,1)S(1)}, u32[]{:S(2)}, u32[]{:S(2)}) async-start(f16[32,6,8,128]{3,2,1,0:T(8,128)(2,1)} %bitcast.23), calls=%async_computation.3 | async-start | bytes 786432 | tf_op jit(solution)/shard_map/cond/branch_1_fun/all_to_all | solution.py:232
  52.4 0.6 %copy-start.3 = (f32[8,2,512]{2,1,0:T(2,128)}, f32[8,2,512]{2,1,0:T(2,128)S(1)}, u32[]{:S(2)}) copy-start(f32[8,2,512]{2,1,0:T(2,128)S(1)} %get-tuple-element.325) | copy-start | bytes 98308
